TPU v7x, 256 devices: a whole 4x4x8 slice. The times are simulated.
256 devices in a mesh: segment: 16 (over x, y), mp: 16 (over z, core).
Axes of the slice: x: 4, y: 4, z: 8, core: 2. Of those that a mesh axis runs over, the one named last changes fastest.
Arguments:
- noise_init: float32 [8192, 64], P('segment'), may hold values from -6 to 6
- step_noise: float32 [4, 8192, 64], P(None, 'segment'), may hold values from -6 to 6
- assign: int32 [128], P('segment'), may hold values from 0 to 31
- slot_map: int32 [128], replicated, may hold values from 0 to 255, as said below
- prompt_embed: bfloat16 [32, 1536], P('segment', 'mp'), may hold values from -6 to 6
- time_vec: bfloat16 [1536], P('mp'), may hold values from -6 to 6
- w_in: bfloat16 [64, 1536], P('segment', 'mp'), may hold values from -0.75 to 0.75
- ln_gain: bfloat16 [1536], P('mp'), may hold values from 0.099609375 to 1.8984375
- w_up: bfloat16 [1536, 6144], P('segment', 'mp'), may hold values from -0.15625 to 0.15625
- w_down: bfloat16 [6144, 1536], P('mp', 'segment'), may hold values from -0.109375 to 0.109375
- w_out: bfloat16 [1536, 64], P('mp', 'segment'), may hold values from -0.15625 to 0.15625
- conv_in_w: bfloat16 [3, 3, 16, 512], replicated, may hold values from -0.5 to 0.5
- gn_gain: float32 [512], replicated, may hold values from 0.1 to 1.9
- conv_mid_w: bfloat16 [3, 3, 512, 512], replicated, may hold values from -0.09375 to 0.09375
Outputs:
- latents: float32 [8192, 64], P('segment')
- decoded: bfloat16 [256, 2, 128, 512], P('segment', None, 'mp')
Inputs may be any that keep to these rules, and one draw needn't show every extreme that they name: `slot_map`: different samples have different slots. Decoder section d owns slots d * 16 to (d + 1) * 16 - 1; in every draw some section has all of its 16 slots filled, and slots 0 and 255 are used.
All inputs are finite; a program needn't handle non-finite values.
Results may differ from a plain program's by a relative error of at most 0.015.
Values may be sent and summed in bfloat16 or wider, within the bound.
A program may use at most 64 MiB of HBM per device.

v0:
```python
import math
import jax
import jax.numpy as jnp
from jax import lax
from jax.sharding import PartitionSpec as P

LAT_CH = 16
VC = 512
GROUPS = 32
STEPS = 4
NOISE_SCALE = 0.5
LATENT_SCALE = 1.0 / 1.5305
EPSILON = 1e-06


def split_up(value, dim, devices):
    before, after = (value.shape[:dim], value.shape[dim + 1 :])
    return jnp.moveaxis(value.reshape(*before, devices, -1, *after), dim, 0)


def sum_at_owner(value, axis, dim):
    blocks = split_up(value, dim, lax.axis_size(axis))
    arrived = lax.all_to_all(blocks, axis, split_axis=0, concat_axis=0, tiled=True)
    return arrived.astype(jnp.float32).sum(axis=0)


def sent_to_all(value, axis):
    copies = jnp.broadcast_to(value, (lax.axis_size(axis), *value.shape))
    return lax.all_to_all(copies, axis, split_axis=0, concat_axis=0, tiled=True)


def taken_together(value, axis):
    return sent_to_all(value, axis).astype(jnp.float32).sum(axis=0)


def joined_along(blocks, dim):
    blocks = jnp.moveaxis(blocks, 0, dim)
    lengths = blocks.shape
    return blocks.reshape(*lengths[:dim], lengths[dim] * lengths[dim + 1], *lengths[dim + 2 :])


def gathered_copies(value, axis, dim):
    return joined_along(sent_to_all(value, axis), dim)


def conv_rows(padded, weight, col_count):
    accumulated = None
    for row_shift in range(3):
        for col_shift in range(3):
            window = padded[:, row_shift : row_shift + 2, col_shift : col_shift + col_count, :]
            product = jnp.einsum(
                "nrcv,vw->nrcw",
                window,
                weight[row_shift, col_shift],
                preferred_element_type=jnp.float32,
            )
            accumulated = product if accumulated is None else accumulated + product
    return accumulated


def decode_tile(latent_tile, mp_index, tile_cols, image_cols, conv_in_w, gn_gain, conv_mid_w):
    slot_rows = latent_tile.shape[0]
    padded = jnp.pad(latent_tile.astype(jnp.bfloat16), ((0, 0), (1, 1), (0, 0), (0, 0)))
    first_wide = conv_rows(padded, conv_in_w, tile_cols + 2)
    conv_first = first_wide[:, :, 1 : tile_cols + 1, :]
    per_group = VC // GROUPS
    grouped = conv_first.reshape(slot_rows, 2 * tile_cols, GROUPS, per_group)
    group_sum, group_square = lax.psum(
        (jnp.sum(grouped, axis=(1, 3)), jnp.sum(grouped * grouped, axis=(1, 3))), "mp"
    )
    entries = 2 * image_cols * per_group
    average = group_sum / entries
    variance = jnp.maximum(group_square / entries - average * average, 0.0)
    inv_spread = lax.rsqrt(variance + EPSILON)
    columns = mp_index * tile_cols - 1 + jnp.arange(tile_cols + 2, dtype=jnp.int32)
    inside = (columns >= 0) & (columns < image_cols)
    col_count = first_wide.shape[2]
    shaped = first_wide.reshape(slot_rows, 2, col_count, GROUPS, per_group)
    shaped = (shaped - average[:, None, None, :, None]) * inv_spread[:, None, None, :, None]
    act_wide = jnp.where(
        inside[None, None, :, None],
        jax.nn.silu(shaped.reshape(slot_rows, 2, col_count, VC) * gn_gain),
        0.0,
    ).astype(jnp.bfloat16)
    act_padded = jnp.pad(act_wide, ((0, 0), (1, 1), (0, 0), (0, 0)))
    return (conv_first + conv_rows(act_padded, conv_mid_w, tile_cols)).astype(jnp.bfloat16)


def full_front(
    latent_state,
    w_in_full,
    prompt_cond,
    time_full,
    gain_full,
    time_now,
    samples_here,
    tok_sample,
    tok_group,
):
    embedded = jnp.dot(
        latent_state.astype(jnp.bfloat16), w_in_full, preferred_element_type=jnp.float32
    )
    hidden_in = (embedded.reshape(samples_here, tok_sample, -1) + prompt_cond[:, None, :]).reshape(
        tok_group, -1
    ) + time_now * time_full.astype(jnp.float32)
    average = jnp.mean(hidden_in, axis=-1, keepdims=True)
    centered = hidden_in - average
    variance = jnp.mean(centered * centered, axis=-1, keepdims=True)
    normed = (centered * lax.rsqrt(variance + EPSILON) * gain_full.astype(jnp.float32)).astype(
        jnp.bfloat16
    )
    return (hidden_in, normed)


def per_device(
    noise_init,
    step_noise,
    assign,
    slot_map,
    prompt_embed,
    time_vec,
    w_in,
    ln_gain,
    w_up,
    w_down,
    w_out,
    conv_in_w,
    gn_gain,
    conv_mid_w,
):
    mp_count = lax.axis_size("mp")
    mp_index = lax.axis_index("mp")
    segment_index = lax.axis_index("segment")
    w_in_rows, w_up_rows, w_down_cols, w_out_cols, prompt_rows = (
        lax.all_gather(w_in, "segment", axis=0, tiled=True),
        lax.all_gather(w_up, "segment", axis=0, tiled=True),
        lax.all_gather(w_down, "segment", axis=1, tiled=True),
        lax.all_gather(w_out, "segment", axis=1, tiled=True),
        lax.all_gather(prompt_embed, "segment", axis=0, tiled=True),
    )
    samples_here = assign.shape[0]
    tok_group = noise_init.shape[0]
    tok_sample = tok_group // samples_here
    prompt_count = prompt_rows.shape[0]
    choose = (assign[:, None] == jnp.arange(prompt_count, dtype=jnp.int32)[None, :]).astype(
        jnp.bfloat16
    )
    step_size = 1.0 / STEPS
    noise_gain = NOISE_SCALE * math.sqrt(step_size)
    latent_state = noise_init
    w_in_full, prompt_full, time_full, gain_full = (
        lax.all_gather(w_in_rows, "mp", axis=1, tiled=True),
        lax.all_gather(prompt_rows, "mp", axis=1, tiled=True),
        lax.all_gather(time_vec, "mp", axis=0, tiled=True),
        lax.all_gather(ln_gain, "mp", axis=0, tiled=True),
    )
    prompt_cond = jnp.dot(choose, prompt_full, preferred_element_type=jnp.float32)
    feat_width = w_out_cols.shape[0]
    for step_index in range(STEPS):
        time_now = 1.0 - step_index * step_size
        hidden_in, normed = full_front(
            latent_state,
            w_in_full,
            prompt_cond,
            time_full,
            gain_full,
            time_now,
            samples_here,
            tok_sample,
            tok_group,
        )
        act = jax.nn.gelu(
            jnp.dot(normed, w_up_rows, preferred_element_type=jnp.float32), approximate=True
        ).astype(jnp.bfloat16)
        mlp_share = sum_at_owner(
            jnp.dot(act, w_down_cols, preferred_element_type=jnp.float32).astype(jnp.bfloat16),
            "mp",
            1,
        )
        hidden_part = lax.dynamic_slice_in_dim(hidden_in, mp_index * feat_width, feat_width, 1)
        partial_vel = jnp.dot(
            (hidden_part + mlp_share).astype(jnp.bfloat16),
            w_out_cols,
            preferred_element_type=jnp.float32,
        )
        velocity = taken_together(partial_vel.astype(jnp.bfloat16), "mp").astype(jnp.float32)
        latent_state = latent_state - step_size * velocity + noise_gain * step_noise[step_index]
    image_cols = 2 * tok_sample
    tile_cols = image_cols // mp_count
    images = (
        latent_state.reshape(samples_here, tok_sample, 2, 2, LAT_CH)
        .transpose(0, 2, 1, 3, 4)
        .reshape(samples_here, 2, image_cols, LAT_CH)
        * LATENT_SCALE
    )
    widened = jnp.pad(images, ((0, 0), (0, 0), (2, 2), (0, 0)))
    latent_tile = lax.dynamic_slice_in_dim(widened, mp_index * tile_cols, tile_cols + 4, 2)
    slot_count = 2 * samples_here
    first_slot = segment_index * slot_count
    slot_ids = first_slot + jnp.arange(slot_count, dtype=jnp.int32)
    own_feats = decode_tile(
        latent_tile, mp_index, tile_cols, image_cols, conv_in_w, gn_gain, conv_mid_w
    )
    slot_picks = (slot_map[None, :] == slot_ids[:, None]).astype(jnp.bfloat16)
    flat_feats = own_feats.reshape(samples_here, -1)
    placed = jnp.dot(
        slot_picks, gathered_copies(flat_feats, "segment", 0), preferred_element_type=jnp.float32
    )
    decoded = placed.astype(jnp.bfloat16).reshape(slot_count, 2, tile_cols, VC)
    return (latent_state, decoded)


def solution(mesh):
    return jax.shard_map(
        per_device,
        mesh=mesh,
        in_specs=(
            P("segment", None),
            P(None, "segment", None),
            P("segment"),
            P(),
            P("segment", "mp"),
            P("mp"),
            P("segment", "mp"),
            P("mp"),
            P("segment", "mp"),
            P("mp", "segment"),
            P("mp", "segment"),
            P(),
            P(),
            P(),
        ),
        out_specs=(P("segment", None), P("segment", None, "mp", None)),
        check_vma=False,
    )
```

profile of v0, /device:TPU:8, one launch (start us, length us, event | category | flops | bytes accessed | tf_op | source)
XLA Modules:
  0.0 554.9 jit_solution(1239499764776693210)
XLA Ops:
  12.3 29.7 %all-reduce.6 = (bf16[1536]{0:T(1024)(128)(2,1)S(1)}, bf16[1536]{0:T(1024)(128)(2,1)S(1)}) all-reduce(bf16[1536]{0:T(1024)(128)(2,1)S(1)} %dynamic-update-slice, bf16[1536]{0:T(1024)(128)(2,1)S(1)} %dynamic-update-slice.1), channel_id=1, replica_groups=mesh['segment'=16,'mp'=16] {'mp'}, use_global_device_ids=true, to_apply=%add.3 | all-reduce | flops 3072 | bytes 12288
  42.1 22.8 %all-gather = bf16[16,4,96]{2,1,0:T(4,128)(2,1)S(1)} all-gather(bf16[1,4,96]{2,1,0:T(4,128)(2,1)} %bitcast.242), channel_id=1, replica_groups=mesh['segment'=16,'mp'=16] {'segment'}, dimensions={0}, use_global_device_ids=true | all-gather | bytes 13056 | tf_op jit(solution)/shard_map/all_gather | solution.py:135
  64.9 14.9 %all-gather.1 = bf16[16,96,64]{1,2,0:T(8,128)(2,1)S(1)} all-gather(bf16[1,96,64]{1,2,0:T(8,128)(2,1)S(1)} %bitcast.240), channel_id=1, replica_groups=mesh['segment'=16,'mp'=16] {'mp'}, dimensions={0}, use_global_device_ids=true | all-gather | bytes 208896 | tf_op jit(solution)/shard_map/all_gather | solution.py:152
  80.2 18.4 %all-gather.2 = bf16[16,2,96]{2,1,0:T(2,128)(2,1)S(1)} all-gather(bf16[1,2,96]{2,1,0:T(2,128)(2,1)} %bitcast.244), channel_id=1, replica_groups=mesh['segment'=16,'mp'=16] {'segment'}, dimensions={0}, use_global_device_ids=true | all-gather | bytes 6528 | tf_op jit(solution)/shard_map/all_gather | solution.py:139
  98.6 16.4 %all-gather.3 = bf16[16,96,32]{1,2,0:T(8,128)(2,1)S(1)} all-gather(bf16[1,96,32]{1,2,0:T(8,128)(2,1)S(1)} %bitcast.241), channel_id=1, replica_groups=mesh['segment'=16,'mp'=16] {'mp'}, dimensions={0}, use_global_device_ids=true | all-gather | bytes 104448 | tf_op jit(solution)/shard_map/all_gather | solution.py:153
  116.1 1.6 fusion.158
  118.2 4.8 convolution_convert_fusion.4
  123.0 2.6 copy.43
  125.6 4.4 all-to-all-start
  130.0 22.3 %all-gather.4 = bf16[16,4,96]{2,1,0:T(4,128)(2,1)S(1)} all-gather(bf16[1,4,96]{2,1,0:T(4,128)(2,1)S(1)} %bitcast.243), channel_id=1, replica_groups=mesh['segment'=16,'mp'=16] {'segment'}, dimensions={0}, use_global_device_ids=true | all-gather | bytes 13056 | tf_op jit(solution)/shard_map/all_gather | solution.py:138
  152.3 15.5 %all-to-all-done = bf16[16,512,96]{1,2,0:T(8,128)(2,1)} async-done(((bf16[16,512,96]{1,2,0:T(8,128)(2,1)}), bf16[16,512,96]{1,2,0:T(8,128)(2,1)}, u32[]{:S(2)}, u32[]{:S(2)}) %all-to-all-start) | async-done | bytes 1572896 | tf_op jit(solution)/shard_map/all_to_all | solution.py:23
  167.8 2.3 convert_reduce_fusion.3
  170.2 1.8 copy.44
  174.3 4.8 all-to-all-start.1
  179.1 1.3 convert_multiply_fusion.1
  180.4 25.4 %all-to-all-done.1 = bf16[16,512,64]{1,2,0:T(8,128)(2,1)S(1)} async-done(((bf16[16,512,64]{1,2,0:T(8,128)(2,1)}), bf16[16,512,64]{1,2,0:T(8,128)(2,1)S(1)}, u32[]{:S(2)}, u32[]{:S(2)}) %all-to-all-start.1) | async-done | bytes 1048608 | tf_op jit(solution)/shard_map/all_to_all | solution.py:29
  205.9 1.6 fusion.159
  208.3 4.8 convolution_convert_fusion.3
  213.0 2.6 copy.45
  215.6 43.3 %all_to_all.45 = bf16[16,512,96]{1,2,0:T(8,128)(2,1)S(1)} all-to-all(bf16[16,512,96]{1,2,0:T(8,128)(2,1)} %bitcast.229), channel_id=1, replica_groups=mesh['segment'=16,'mp'=16] {'mp'}, dimensions={0} | all-to-all | bytes 3145728 | tf_op jit(solution)/shard_map/all_to_all | solution.py:23
  259.8 1.8 copy.46
  261.5 1.3 convolution_convert_fusion.7
  262.9 31.3 %all_to_all.46 = bf16[16,512,64]{1,2,0:T(8,128)(2,1)S(1)} all-to-all(bf16[16,512,64]{1,2,0:T(8,128)(2,1)S(1)} %broadcast_in_dim.19), channel_id=1, replica_groups=mesh['segment'=16,'mp'=16] {'mp'}, dimensions={0} | all-to-all | bytes 2097152 | tf_op jit(solution)/shard_map/all_to_all | solution.py:29
  295.6 4.8 convolution_convert_fusion.2
  300.4 2.6 copy.47
  303.0 42.8 %all_to_all.47 = bf16[16,512,96]{1,2,0:T(8,128)(2,1)S(1)} all-to-all(bf16[16,512,96]{1,2,0:T(8,128)(2,1)} %bitcast.230), channel_id=1, replica_groups=mesh['segment'=16,'mp'=16] {'mp'}, dimensions={0} | all-to-all | bytes 3145728 | tf_op jit(solution)/shard_map/all_to_all | solution.py:23
  346.7 1.8 copy.48
  349.8 31.1 %all_to_all.48 = bf16[16,512,64]{1,2,0:T(8,128)(2,1)S(1)} all-to-all(bf16[16,512,64]{1,2,0:T(8,128)(2,1)S(1)} %broadcast_in_dim.20), channel_id=1, replica_groups=mesh['segment'=16,'mp'=16] {'mp'}, dimensions={0} | all-to-all | bytes 2097152 | tf_op jit(solution)/shard_map/all_to_all | solution.py:29
  381.1 1.6 fusion.161
  383.2 4.8 convolution_convert_fusion.1
  387.9 2.6 copy.49
  390.5 42.8 %all_to_all.49 = bf16[16,512,96]{1,2,0:T(8,128)(2,1)S(1)} all-to-all(bf16[16,512,96]{1,2,0:T(8,128)(2,1)} %bitcast.231), channel_id=1, replica_groups=mesh['segment'=16,'mp'=16] {'mp'}, dimensions={0} | all-to-all | bytes 3145728 | tf_op jit(solution)/shard_map/all_to_all | solution.py:23
  434.2 1.8 copy.50
  438.4 4.1 all-to-all-start.7
  442.5 26.6 %all-to-all-done.7 = bf16[16,512,64]{1,2,0:T(8,128)(2,1)S(1)} async-done(((bf16[16,512,64]{1,2,0:T(8,128)(2,1)}), bf16[16,512,64]{1,2,0:T(8,128)(2,1)S(1)}, u32[]{:S(2)}, u32[]{:S(2)}) %all-to-all-start.7) | async-done | bytes 1048608 | tf_op jit(solution)/shard_map/all_to_all | solution.py:29
  473.0 25.8 %all-reduce.5 = (f32[8,32]{1,0:T(8,128)S(1)}, f32[8,32]{1,0:T(8,128)S(1)}) all-reduce(f32[8,32]{1,0:T(8,128)S(1)} %reduce_sum.197, f32[8,32]{1,0:T(8,128)S(1)} %reduce_sum.194), channel_id=1, replica_groups=mesh['segment'=16,'mp'=16] {'mp'}, use_global_device_ids=true, to_apply=%region_21.22 | all-reduce | flops 512 | bytes 4096 | tf_op jit(solution)/shard_map/psum | solution.py:68
  499.4 1.3 fusion.64
  500.7 1.3 convolution_add_fusion.15
  502.0 1.3 convolution_add_fusion.14
  503.3 1.3 convolution_add_fusion.13
  504.6 1.3 convolution_add_fusion.12
  505.8 1.3 convolution_add_fusion.11
  507.1 1.3 convolution_add_fusion.10
  508.4 1.3 convolution_add_fusion.9
  509.7 1.3 fusion.23
  511.1 1.6 broadcast_in_dim.24
  512.6 7.5 %all-to-all-start.8 = ((bf16[16,8,8192]{2,1,0:T(8,128)(2,1)}), bf16[16,8,8192]{2,1,0:T(8,128)(2,1)S(1)}, u32[]{:S(2)}, u32[]{:S(2)}) async-start(bf16[16,8,8192]{2,1,0:T(8,128)(2,1)} %broadcast_in_dim.24), calls=%async_computation.8 | async-start | bytes 4194304 | tf_op jit(solution)/shard_map/all_to_all | solution.py:29
  520.2 26.7 %all-to-all-done.8 = bf16[16,8,8192]{2,1,0:T(8,128)(2,1)S(1)} async-done(((bf16[16,8,8192]{2,1,0:T(8,128)(2,1)}), bf16[16,8,8192]{2,1,0:T(8,128)(2,1)S(1)}, u32[]{:S(2)}, u32[]{:S(2)}) %all-to-all-start.8) | async-done | bytes 2097184 | tf_op jit(solution)/shard_map/all_to_all | solution.py:29
  (107 shorter events, 23.6 us)
Async XLA Ops:
  7.2 111.0 %all-gather.10.cloned.1.call-start = ((), (), s32[]{:S(2)}) async-start(), calls=%async_computation.10 | async-start | bytes 1253376 | tf_op jit(solution)/shard_map/all_gather | solution.py:137
  7.9 110.3 %all-gather.8.cloned.1.call-start = ((), (), s32[]{:S(2)}) async-start(), calls=%async_computation.9 | async-start | bytes 1253376 | tf_op jit(solution)/shard_map/all_gather | solution.py:136
  42.0 22.8 %copy-start.9 = (bf16[1536]{0:T(1024)(128)(2,1)}, bf16[1536]{0:T(1024)(128)(2,1)S(1)}, u32[]{:S(2)}) copy-start(bf16[1536]{0:T(1024)(128)(2,1)S(1)} %get-tuple-element.6) | copy-start | bytes 9220
  115.2 3.0 copy-start.10
  123.0 7.0 %copy-start.14 = (bf16[96,4]{0,1:T(4,128)(2,1)S(1)}, bf16[96,4]{0,1:T(4,128)(2,1)}, u32[]{:S(2)}) copy-start(bf16[96,4]{0,1:T(4,128)(2,1)} %param.24) | copy-start | bytes 2308
  125.6 42.3 %all-to-all-start = ((bf16[16,512,96]{1,2,0:T(8,128)(2,1)}), bf16[16,512,96]{1,2,0:T(8,128)(2,1)}, u32[]{:S(2)}, u32[]{:S(2)}) async-start(bf16[16,512,96]{1,2,0:T(8,128)(2,1)} %bitcast.228), calls=%async_computation | async-start | bytes 3145728 | tf_op jit(solution)/shard_map/all_to_all | solution.py:23
  170.2 35.7 %copy-start.2 = (f32[512,64]{0,1:T(8,128)S(1)}, f32[512,64]{0,1:T(8,128)}, u32[]{:S(2)}) copy-start(f32[512,64]{0,1:T(8,128)} %param.14) | copy-start | bytes 393220
  174.3 31.5 %all-to-all-start.1 = ((bf16[16,512,64]{1,2,0:T(8,128)(2,1)}), bf16[16,512,64]{1,2,0:T(8,128)(2,1)S(1)}, u32[]{:S(2)}, u32[]{:S(2)}) async-start(bf16[16,512,64]{1,2,0:T(8,128)(2,1)} %broadcast_in_dim.18), calls=%async_computation.1 | async-start | bytes 2097152 | tf_op jit(solution)/shard_map/all_to_all | solution.py:29
  205.9 1.7 copy-start.6
  207.6 0.7 copy-start.11
  261.5 32.8 %copy-start = (f32[4,512,64]{1,2,0:T(8,128)S(1)}, f32[4,512,64]{1,2,0:T(8,128)}, u32[]{:S(2)}) copy-start(f32[4,512,64]{1,2,0:T(8,128)} %param.15) | copy-start | bytes 1572868
  261.5 32.8 %copy-start.3 = (f32[512,64]{0,1:T(8,128)S(1)}, f32[512,64]{0,1:T(8,128)}, u32[]{:S(2)}) copy-start(f32[512,64]{0,1:T(8,128)} %param.14) | copy-start | bytes 393220
  261.5 32.8 %copy-start.7 = (f32[512,64]{0,1:T(8,128)S(1)}, f32[512,64]{0,1:T(8,128)}, u32[]{:S(2)}) copy-start(f32[512,64]{0,1:T(8,128)} %copy-done.6) | copy-start | bytes 393220
  381.0 1.7 copy-start.4
  381.1 2.1 copy-start.12
  434.2 35.0 %copy-start.5 = (f32[512,64]{0,1:T(8,128)S(1)}, f32[512,64]{0,1:T(8,128)}, u32[]{:S(2)}) copy-start(f32[512,64]{0,1:T(8,128)} %copy-done.4) | copy-start | bytes 393220
  437.3 32.0 %copy-start.1 = (f32[4,512,64]{1,2,0:T(8,128)S(1)}, f32[4,512,64]{1,2,0:T(8,128)}, u32[]{:S(2)}) copy-start(f32[4,512,64]{1,2,0:T(8,128)} %param.15) | copy-start | bytes 1572868
  437.3 33.3 %copy-start.8 = (bf16[3,3,16,512]{3,2,1,0:T(8,128)(2,1)S(1)}, bf16[3,3,16,512]{3,2,1,0:T(8,128)(2,1)}, u32[]{:S(2)}) copy-start(bf16[3,3,16,512]{3,2,1,0:T(8,128)(2,1)} %param.25) | copy-start | bytes 442372
  438.4 30.7 %all-to-all-start.7 = ((bf16[16,512,64]{1,2,0:T(8,128)(2,1)}), bf16[16,512,64]{1,2,0:T(8,128)(2,1)S(1)}, u32[]{:S(2)}, u32[]{:S(2)}) async-start(bf16[16,512,64]{1,2,0:T(8,128)(2,1)} %broadcast_in_dim.21), calls=%async_computation.7 | async-start | bytes 2097152 | tf_op jit(solution)/shard_map/all_to_all | solution.py:29
  471.6 27.6 %copy-start.13 = (f32[512]{0:T(512)S(1)}, f32[512]{0:T(512)}, u32[]{:S(2)}) copy-start(f32[512]{0:T(512)} %param.26) | copy-start | bytes 6148
  511.1 35.8 %copy-start.15 = (s32[128]{0:T(128)S(1)}, s32[128]{0:T(128)}, u32[]{:S(2)}) copy-start(s32[128]{0:T(128)} %param.17) | copy-start | bytes 1540
  512.6 34.2 %all-to-all-start.8 = ((bf16[16,8,8192]{2,1,0:T(8,128)(2,1)}), bf16[16,8,8192]{2,1,0:T(8,128)(2,1)S(1)}, u32[]{:S(2)}, u32[]{:S(2)}) async-start(bf16[16,8,8192]{2,1,0:T(8,128)(2,1)} %broadcast_in_dim.24), calls=%async_computation.8 | async-start | bytes 4194304 | tf_op jit(solution)/shard_map/all_to_all | solution.py:29
Sparse Core Ops, SparseCore 0:
  10.5 50.6 all-gather.9
  63.7 47.5 all-gather.7
where the time goes:
time: 557 us; the launch traced here: 555 us
  blocking collectives  342 us (61%)
  waiting for transfers between devices  95.6 us (17%)
  matrix products  44.1 us (8%)
  local copies, waits for them, and re-layouts  27.4 us (5%)
  starting transfers between devices  20.8 us (4%)
  between operations  15.3 us (3%)
  other arithmetic  10 us (2%)
    all_to_all x3, blocking collectives, sum_at_owner(): lax.all_to_all(blocks, axis, split_axis=0, concat_axis=0, tiled=True)  129 us
    all_to_all x3, waiting for transfers between devices, sent_to_all(): return lax.all_to_all(copies, axis, split_axis=0, concat_axis=0, tiled=True)  78.7 us
    all_to_all x2, blocking collectives, sent_to_all(): return lax.all_to_all(copies, axis, split_axis=0, concat_axis=0, tiled=True)  62.4 us
    unnamed x1, blocking collectives  29.7 us
    psum x1, blocking collectives, decode_tile(): lax.psum((jnp.sum(grouped, axis=(1, 3)), jnp.sum(grouped * grouped, axis=...  25.8 us
    all_gather x1, blocking collectives, per_device(): lax.all_gather(w_in, 'segment', axis=0, tiled=True)  22.8 us
    all_gather x1, blocking collectives, per_device(): lax.all_gather(w_out, 'segment', axis=1, tiled=True)  22.3 us
    dot_general x4, matrix products, per_device(): jnp.dot(act, w_down_cols, preferred_element_type=jnp.float32)  19 us
  transfers between devices with their start and end apart: 6, of which 4 were waited for; matrix products, arithmetic and copies ran while one was open for 1% of the time, Pallas kernels for 0%

commit v1 on v0

--- a/solution.py
+++ b/solution.py
@@ -11,6 +11,28 @@
 NOISE_SCALE = 0.5
 LATENT_SCALE = 1.0 / 1.5305
 EPSILON = 1e-06
+
+
+def joined_along_2(blocks, dim):
+    shape = list(blocks.shape[1:])
+    shape[dim] *= blocks.shape[0]
+    return jnp.moveaxis(blocks, 0, dim).reshape(shape)
+
+
+def ring_gather(array, axis, dim):
+    length = lax.axis_size(axis)
+    pairs = [(i, (i + 1) % length) for i in range(length)]
+    back = [(b, a) for a, b in pairs]
+    lower, upper = ([], [])
+    for step in range(length - 1):
+        if step % 2 == 0:
+            lower.append(lax.ppermute(lower[-1] if lower else array, axis, pairs))
+        else:
+            upper.append(lax.ppermute(upper[-1] if upper else array, axis, back))
+    pieces = jnp.stack([*lower[::-1], array, *upper])
+    shift = lax.axis_index(axis) - len(lower)
+    pieces = pieces[(jnp.arange(length) - shift) % length]
+    return joined_along_2(pieces, dim)
 
 
 def split_up(value, dim, devices):
@@ -149,7 +171,7 @@
     noise_gain = NOISE_SCALE * math.sqrt(step_size)
     latent_state = noise_init
     w_in_full, prompt_full, time_full, gain_full = (
-        lax.all_gather(w_in_rows, "mp", axis=1, tiled=True),
+        ring_gather(w_in_rows, "mp", 1),
         lax.all_gather(prompt_rows, "mp", axis=1, tiled=True),
         lax.all_gather(time_vec, "mp", axis=0, tiled=True),
         lax.all_gather(ln_gain, "mp", axis=0, tiled=True),

time: 557 us -> 587 us (1.054)
  blocking collectives: 342 us -> 325 us
  starting transfers between devices: 20.8 us -> 36.8 us
  local copies, waits for them, and re-layouts: 27.4 us -> 41.4 us
  other arithmetic: 10 us -> 19.8 us
  waiting for transfers between devices: 95.6 us -> 103 us
    ppermute x0 -> x15, starting transfers between devices: none -> 15.4 us  [the longest x7 15 us: ring_gather(): upper.append(lax.ppermute(upper[-1] if upper else array, axis, back))]
    all_gather x1 -> x0, blocking collectives: 14.9 us -> none  [per_device(): lax.all_gather(w_in_rows, 'mp', axis=1, tiled=True)]
    ppermute x0 -> x15, waiting for transfers between devices: none -> 9.37 us  [the longest x8 7.32 us: ring_gather(): lower.append(lax.ppermute(lower[-1] if lower else array, axis, pairs))]
    reshape x0 -> x5, local copies, waits for them, and re-layouts: none -> 8.61 us  [the longest x3 7.13 us: full_front(): (embedded.reshape(samples_here, tok_sample, -1) + prompt_cond[:, None, :]...]
    reduce_sum x4 -> x0, local copies, waits for them, and re-layouts: 7.12 us -> none  [sum_at_owner(): return arrived.astype(jnp.float32).sum(axis=0)]
    unnamed x41 -> x61, local copies, waits for them, and re-layouts: 4.57 us -> 11.5 us
    add x1 -> x3, other arithmetic: 0.06 us -> 6.5 us  [full_front(): (embedded.reshape(samples_here, tok_sample, -1) + prompt_cond[:, None, :]...]
  transfers between devices with their start and end apart: 6 -> 21, of which waited for: 4 -> 10; matrix products, arithmetic and copies ran while one was open for 1% -> 3% of each run, Pallas kernels for 0% -> 0%
where the time goes in v1:
time: 587 us; the launch traced here: 585 us
  blocking collectives  325 us (55%)
  waiting for transfers between devices  103 us (18%)
  matrix products  43.5 us (7%)
  local copies, waits for them, and re-layouts  41.4 us (7%)
  starting transfers between devices  36.8 us (6%)
  other arithmetic  19.8 us (3%)
  between operations  15.4 us (3%)
    all_to_all x3, blocking collectives, sum_at_owner(): lax.all_to_all(blocks, axis, split_axis=0, concat_axis=0, tiled=True)  128 us
    all_to_all x3, waiting for transfers between devices, sent_to_all(): return lax.all_to_all(copies, axis, split_axis=0, concat_axis=0, tiled=True)  77.4 us
    all_to_all x2, blocking collectives, sent_to_all(): return lax.all_to_all(copies, axis, split_axis=0, concat_axis=0, tiled=True)  62.5 us
    unnamed x1, blocking collectives  28 us
    psum x1, blocking collectives, decode_tile(): lax.psum((jnp.sum(grouped, axis=(1, 3)), jnp.sum(grouped * grouped, axis=...  25.8 us
    all_gather x1, blocking collectives, per_device(): lax.all_gather(w_in, 'segment', axis=0, tiled=True)  23.2 us
    all_gather x1, blocking collectives, per_device(): lax.all_gather(w_out, 'segment', axis=1, tiled=True)  22.4 us
    dot_general x4, matrix products, per_device(): jnp.dot(act, w_down_cols, preferred_element_type=jnp.float32)  19.3 us
  transfers between devices with their start and end apart: 21, of which 10 were waited for; matrix products, arithmetic and copies ran while one was open for 3% of the time, Pallas kernels for 0%

profile of v1, /device:TPU:8, one launch (start us, length us, event | category | flops | bytes accessed | tf_op | source)
XLA Modules:
  0.0 585.0 jit_solution(7781824879629960473)
XLA Ops:
  7.9 23.2 %all-gather = bf16[16,4,96]{2,1,0:T(4,128)(2,1)S(1)} all-gather(bf16[1,4,96]{2,1,0:T(4,128)(2,1)} %bitcast.281), channel_id=1, replica_groups=mesh['segment'=16,'mp'=16] {'segment'}, dimensions={0}, use_global_device_ids=true | all-gather | bytes 13056 | tf_op jit(solution)/shard_map/all_gather | solution.py:157
  31.2 4.4 collective-permute-done
  35.5 3.0 collective-permute-start.8
  39.9 2.9 collective-permute-start.9
  44.3 18.4 %all-gather.1 = bf16[16,2,96]{2,1,0:T(2,128)(2,1)S(1)} all-gather(bf16[1,2,96]{2,1,0:T(2,128)(2,1)} %bitcast.283), channel_id=1, replica_groups=mesh['segment'=16,'mp'=16] {'segment'}, dimensions={0}, use_global_device_ids=true | all-gather | bytes 6528 | tf_op jit(solution)/shard_map/all_gather | solution.py:161
  63.2 16.9 %all-gather.2 = bf16[16,96,32]{1,2,0:T(8,128)(2,1)S(1)} all-gather(bf16[1,96,32]{1,2,0:T(8,128)(2,1)S(1)} %bitcast.280), channel_id=1, replica_groups=mesh['segment'=16,'mp'=16] {'mp'}, dimensions={0}, use_global_device_ids=true | all-gather | bytes 104448 | tf_op jit(solution)/shard_map/all_gather | solution.py:175
  80.3 3.2 collective-permute-start.11
  84.9 2.9 collective-permute-start.12
  89.3 2.9 collective-permute-start.13
  96.6 28.0 %all-reduce.6 = (bf16[1536]{0:T(1024)(128)(2,1)S(1)}, bf16[1536]{0:T(1024)(128)(2,1)}) all-reduce(bf16[1536]{0:T(1024)(128)(2,1)S(1)} %dynamic-update-slice, bf16[1536]{0:T(1024)(128)(2,1)S(1)} %dynamic-update-slice.1), channel_id=1, replica_groups=mesh['segment'=16,'mp'=16] {'mp'}, use_global_device_ids=true, to_apply=%add.3 | all-reduce | flops 3072 | bytes 12288
  125.1 2.4 copy.66
  131.7 2.5 fusion.158
  134.7 4.8 convolution_convert_fusion.4
  139.5 2.6 copy.67
  142.2 5.1 all-to-all-start
  147.3 22.4 %all-gather.3 = bf16[16,4,96]{2,1,0:T(4,128)(2,1)S(1)} all-gather(bf16[1,4,96]{2,1,0:T(4,128)(2,1)S(1)} %bitcast.282), channel_id=1, replica_groups=mesh['segment'=16,'mp'=16] {'segment'}, dimensions={0}, use_global_device_ids=true | all-gather | bytes 13056 | tf_op jit(solution)/shard_map/all_gather | solution.py:160
  169.7 15.5 %all-to-all-done = bf16[16,512,96]{1,2,0:T(8,128)(2,1)} async-done(((bf16[16,512,96]{1,2,0:T(8,128)(2,1)}), bf16[16,512,96]{1,2,0:T(8,128)(2,1)}, u32[]{:S(2)}, u32[]{:S(2)}) %all-to-all-start) | async-done | bytes 1572896 | tf_op jit(solution)/shard_map/all_to_all | solution.py:45
  185.2 1.6 convert_reduce_fusion.3
  188.1 4.8 all-to-all-start.1
  195.4 24.2 %all-to-all-done.1 = bf16[16,512,64]{1,2,0:T(8,128)(2,1)S(1)} async-done(((bf16[16,512,64]{1,2,0:T(8,128)(2,1)}), bf16[16,512,64]{1,2,0:T(8,128)(2,1)S(1)}, u32[]{:S(2)}, u32[]{:S(2)}) %all-to-all-start.1) | async-done | bytes 1048608 | tf_op jit(solution)/shard_map/all_to_all | solution.py:51
  221.5 1.5 add_reduce_fusion.2
  228.2 2.4 copy.69
  230.6 2.2 broadcast_add_fusion.2
  232.7 1.7 copy-done.1
  234.4 4.8 convolution_convert_fusion.3
  239.2 1.7 copy.70
  240.9 43.1 %all_to_all.45 = bf16[16,512,96]{1,2,0:T(8,128)(2,1)S(1)} all-to-all(bf16[16,512,96]{1,2,0:T(8,128)(2,1)S(1)} %bitcast.262), channel_id=1, replica_groups=mesh['segment'=16,'mp'=16] {'mp'}, dimensions={0} | all-to-all | bytes 3145728 | tf_op jit(solution)/shard_map/all_to_all | solution.py:45
  285.5 31.2 %all_to_all.46 = bf16[16,512,64]{1,2,0:T(8,128)(2,1)S(1)} all-to-all(bf16[16,512,64]{1,2,0:T(8,128)(2,1)S(1)} %broadcast_in_dim.19), channel_id=1, replica_groups=mesh['segment'=16,'mp'=16] {'mp'}, dimensions={0} | all-to-all | bytes 2097152 | tf_op jit(solution)/shard_map/all_to_all | solution.py:51
  319.1 2.4 copy.72
  321.4 2.2 broadcast_add_fusion.1
  323.6 1.7 copy-done.2
  325.3 4.8 convolution_convert_fusion.2
  330.1 1.7 copy.73
  331.8 42.5 %all_to_all.47 = bf16[16,512,96]{1,2,0:T(8,128)(2,1)S(1)} all-to-all(bf16[16,512,96]{1,2,0:T(8,128)(2,1)S(1)} %bitcast.263), channel_id=1, replica_groups=mesh['segment'=16,'mp'=16] {'mp'}, dimensions={0} | all-to-all | bytes 3145728 | tf_op jit(solution)/shard_map/all_to_all | solution.py:45
  375.8 31.3 %all_to_all.48 = bf16[16,512,64]{1,2,0:T(8,128)(2,1)S(1)} all-to-all(bf16[16,512,64]{1,2,0:T(8,128)(2,1)S(1)} %broadcast_in_dim.20), channel_id=1, replica_groups=mesh['segment'=16,'mp'=16] {'mp'}, dimensions={0} | all-to-all | bytes 2097152 | tf_op jit(solution)/shard_map/all_to_all | solution.py:51
  408.9 1.5 add_reduce_fusion
  411.1 2.4 copy.75
  413.5 2.2 broadcast_add_fusion
  415.7 1.7 copy-done
  417.3 4.8 convolution_convert_fusion.1
  422.2 1.7 copy.76
  423.9 42.5 %all_to_all.49 = bf16[16,512,96]{1,2,0:T(8,128)(2,1)S(1)} all-to-all(bf16[16,512,96]{1,2,0:T(8,128)(2,1)S(1)} %bitcast.264), channel_id=1, replica_groups=mesh['segment'=16,'mp'=16] {'mp'}, dimensions={0} | all-to-all | bytes 3145728 | tf_op jit(solution)/shard_map/all_to_all | solution.py:45
  468.8 4.2 all-to-all-start.7
  473.0 26.6 %all-to-all-done.7 = bf16[16,512,64]{1,2,0:T(8,128)(2,1)S(1)} async-done(((bf16[16,512,64]{1,2,0:T(8,128)(2,1)}), bf16[16,512,64]{1,2,0:T(8,128)(2,1)S(1)}, u32[]{:S(2)}, u32[]{:S(2)}) %all-to-all-start.7) | async-done | bytes 1048608 | tf_op jit(solution)/shard_map/all_to_all | solution.py:51
  503.5 25.8 %all-reduce.5 = (f32[8,32]{1,0:T(8,128)S(1)}, f32[8,32]{1,0:T(8,128)S(1)}) all-reduce(f32[8,32]{1,0:T(8,128)S(1)} %reduce_sum.197, f32[8,32]{1,0:T(8,128)S(1)} %reduce_sum.194), channel_id=1, replica_groups=mesh['segment'=16,'mp'=16] {'mp'}, use_global_device_ids=true, to_apply=%region_21.22 | all-reduce | flops 512 | bytes 4096 | tf_op jit(solution)/shard_map/psum | solution.py:90
  541.6 1.6 broadcast_in_dim.24
  543.2 7.2 %all-to-all-start.8 = ((bf16[16,8,8192]{2,1,0:T(8,128)(2,1)}), bf16[16,8,8192]{2,1,0:T(8,128)(2,1)S(1)}, u32[]{:S(2)}, u32[]{:S(2)}) async-start(bf16[16,8,8192]{2,1,0:T(8,128)(2,1)} %broadcast_in_dim.24), calls=%async_computation.8 | async-start | bytes 4194304 | tf_op jit(solution)/shard_map/all_to_all | solution.py:51
  550.3 26.6 %all-to-all-done.8 = bf16[16,8,8192]{2,1,0:T(8,128)(2,1)S(1)} async-done(((bf16[16,8,8192]{2,1,0:T(8,128)(2,1)}), bf16[16,8,8192]{2,1,0:T(8,128)(2,1)S(1)}, u32[]{:S(2)}, u32[]{:S(2)}) %all-to-all-start.8) | async-done | bytes 2097184 | tf_op jit(solution)/shard_map/all_to_all | solution.py:51
  (177 shorter events, 54.2 us)
Async XLA Ops:
  7.2 127.5 %all-gather.7.cloned.1.call-start = ((), (), s32[]{:S(2)}) async-start(), calls=%async_computation.9 | async-start | bytes 1253376 | tf_op jit(solution)/shard_map/all_gather | solution.py:158
  7.9 126.8 %all-gather.9.cloned.1.call-start = ((), (), s32[]{:S(2)}) async-start(), calls=%async_computation.10 | async-start | bytes 1253376 | tf_op jit(solution)/shard_map/all_gather | solution.py:159
  31.2 4.4 collective-permute-start
  35.5 4.4 collective-permute-start.1
  35.5 4.4 collective-permute-start.8
  39.9 4.4 collective-permute-start.2
  39.9 22.7 %collective-permute-start.9 = (bf16[64,96]{1,0:T(8,128)(2,1)S(1)}, bf16[64,96]{1,0:T(8,128)(2,1)S(1)}, u32[]{:S(2)}, u32[]{:S(2)}) collective-permute-start(bf16[64,96]{1,0:T(8,128)(2,1)S(1)} %collective-permute-done.8), channel_id=1, source_target_pairs={{1,0},{2,1},{3,2},{4,3},{5,4},{6,5},{7,6},{8,7},{9,8},{10,9},{11,1... | collective-permute-start | bytes 36872 | tf_op jit(solution)/shard_map/ppermute | solution.py:31
  44.3 18.5 %collective-permute-start.3 = (bf16[64,96]{1,0:T(8,128)(2,1)S(1)}, bf16[64,96]{1,0:T(8,128)(2,1)S(1)}, u32[]{:S(2)}, u32[]{:S(2)}) collective-permute-start(bf16[64,96]{1,0:T(8,128)(2,1)S(1)} %collective-permute-done.2), channel_id=1, source_target_pairs={{0,1},{1,2},{2,3},{3,4},{4,5},{5,6},{6,7},{7,8},{8,9},{9,10},{10,1... | collective-permute-start | bytes 36872 | tf_op jit(solution)/shard_map/ppermute | solution.py:29
  62.7 17.6 %collective-permute-start.10 = (bf16[64,96]{1,0:T(8,128)(2,1)S(1)}, bf16[64,96]{1,0:T(8,128)(2,1)S(1)}, u32[]{:S(2)}, u32[]{:S(2)}) collective-permute-start(bf16[64,96]{1,0:T(8,128)(2,1)S(1)} %collective-permute-done.9), channel_id=1, source_target_pairs={{1,0},{2,1},{3,2},{4,3},{5,4},{6,5},{7,6},{8,7},{9,8},{10,9},{11,1... | collective-permute-start | bytes 36872 | tf_op jit(solution)/shard_map/ppermute | solution.py:31
  62.8 20.7 %collective-permute-start.4 = (bf16[64,96]{1,0:T(8,128)(2,1)S(1)}, bf16[64,96]{1,0:T(8,128)(2,1)S(1)}, u32[]{:S(2)}, u32[]{:S(2)}) collective-permute-start(bf16[64,96]{1,0:T(8,128)(2,1)S(1)} %collective-permute-done.3), channel_id=1, source_target_pairs={{0,1},{1,2},{2,3},{3,4},{4,5},{5,6},{6,7},{7,8},{8,9},{9,10},{10,1... | collective-permute-start | bytes 36872 | tf_op jit(solution)/shard_map/ppermute | solution.py:29
  80.3 4.6 collective-permute-start.11
  83.5 4.4 collective-permute-start.5
  84.9 4.4 collective-permute-start.12
  87.8 4.5 collective-permute-start.6
  89.3 38.9 %collective-permute-start.13 = (bf16[64,96]{1,0:T(8,128)(2,1)S(1)}, bf16[64,96]{1,0:T(8,128)(2,1)S(1)}, u32[]{:S(2)}, u32[]{:S(2)}) collective-permute-start(bf16[64,96]{1,0:T(8,128)(2,1)S(1)} %collective-permute-done.12), channel_id=1, source_target_pairs={{1,0},{2,1},{3,2},{4,3},{5,4},{6,5},{7,6},{8,7},{9,8},{10,9},{11,1... | collective-permute-start | bytes 36872 | tf_op jit(solution)/shard_map/ppermute | solution.py:31
  92.3 35.9 %collective-permute-start.7 = (bf16[64,96]{1,0:T(8,128)(2,1)}, bf16[64,96]{1,0:T(8,128)(2,1)}, u32[]{:S(2)}, u32[]{:S(2)}) collective-permute-start(bf16[64,96]{1,0:T(8,128)(2,1)} %collective-permute-done.6), channel_id=1, source_target_pairs={{0,1},{1,2},{2,3},{3,4},{4,5},{5,6},{6,7},{7,8},{8,9},{9,10},{10,1... | collective-permute-start | bytes 36872 | tf_op jit(solution)/shard_map/ppermute | solution.py:29
  124.5 0.6 copy-start.12
  125.1 6.6 %copy-start.6 = (f32[512,64]{0,1:T(8,128)S(1)}, f32[512,64]{0,1:T(8,128)}, u32[]{:S(2)}) copy-start(f32[512,64]{0,1:T(8,128)} %param.14) | copy-start | bytes 393220
  128.2 6.5 %copy-start.13 = (f32[1536]{0:T(1024)}, f32[1536]{0:T(1024)S(1)}, u32[]{:S(2)}) copy-start(f32[1536]{0:T(1024)S(1)} %convert_element_type.130) | copy-start | bytes 18436
  128.2 1.6 collective-permute-start.14
  130.7 0.7 copy-start.3
  139.5 7.7 %copy-start.17 = (bf16[96,4]{0,1:T(4,128)(2,1)S(1)}, bf16[96,4]{0,1:T(4,128)(2,1)}, u32[]{:S(2)}) copy-start(bf16[96,4]{0,1:T(4,128)(2,1)} %param.24) | copy-start | bytes 2308
  142.2 43.0 %all-to-all-start = ((bf16[16,512,96]{1,2,0:T(8,128)(2,1)}), bf16[16,512,96]{1,2,0:T(8,128)(2,1)}, u32[]{:S(2)}, u32[]{:S(2)}) async-start(bf16[16,512,96]{1,2,0:T(8,128)(2,1)} %bitcast.261), calls=%async_computation | async-start | bytes 3145728 | tf_op jit(solution)/shard_map/all_to_all | solution.py:45
  188.1 31.5 %all-to-all-start.1 = ((bf16[16,512,64]{1,2,0:T(8,128)(2,1)}), bf16[16,512,64]{1,2,0:T(8,128)(2,1)S(1)}, u32[]{:S(2)}, u32[]{:S(2)}) async-start(bf16[16,512,64]{1,2,0:T(8,128)(2,1)} %broadcast_in_dim.18), calls=%async_computation.1 | async-start | bytes 2097152 | tf_op jit(solution)/shard_map/all_to_all | solution.py:51
  219.7 1.8 copy-start.7
  232.7 1.7 copy-start.1
  284.0 32.8 %copy-start.4 = (f32[4,512,64]{1,2,0:T(8,128)S(1)}, f32[4,512,64]{1,2,0:T(8,128)}, u32[]{:S(2)}) copy-start(f32[4,512,64]{1,2,0:T(8,128)} %param.15) | copy-start | bytes 1572868
  284.0 32.8 %copy-start.8 = (f32[512,64]{0,1:T(8,128)S(1)}, f32[512,64]{0,1:T(8,128)}, u32[]{:S(2)}) copy-start(f32[512,64]{0,1:T(8,128)} %copy-done.7) | copy-start | bytes 393220
  321.4 3.8 copy-start.14
  323.6 1.7 copy-start.2
  374.3 32.8 %copy-start.9 = (f32[512,64]{0,1:T(8,128)S(1)}, f32[512,64]{0,1:T(8,128)}, u32[]{:S(2)}) copy-start(f32[512,64]{0,1:T(8,128)} %get-tuple-element.11) | copy-start | bytes 393220
  413.5 3.8 copy-start.15
  415.7 1.7 copy-start
  466.4 33.4 %copy-start.5 = (f32[4,512,64]{1,2,0:T(8,128)S(1)}, f32[4,512,64]{1,2,0:T(8,128)}, u32[]{:S(2)}) copy-start(f32[4,512,64]{1,2,0:T(8,128)} %param.15) | copy-start | bytes 1572868
  466.4 33.4 %copy-start.10 = (f32[512,64]{0,1:T(8,128)S(1)}, f32[512,64]{0,1:T(8,128)}, u32[]{:S(2)}) copy-start(f32[512,64]{0,1:T(8,128)} %get-tuple-element.11) | copy-start | bytes 393220
  467.7 33.4 %copy-start.11 = (bf16[3,3,16,512]{3,2,1,0:T(8,128)(2,1)S(1)}, bf16[3,3,16,512]{3,2,1,0:T(8,128)(2,1)}, u32[]{:S(2)}) copy-start(bf16[3,3,16,512]{3,2,1,0:T(8,128)(2,1)} %param.25) | copy-start | bytes 442372
  468.8 30.8 %all-to-all-start.7 = ((bf16[16,512,64]{1,2,0:T(8,128)(2,1)}), bf16[16,512,64]{1,2,0:T(8,128)(2,1)S(1)}, u32[]{:S(2)}, u32[]{:S(2)}) async-start(bf16[16,512,64]{1,2,0:T(8,128)(2,1)} %broadcast_in_dim.21), calls=%async_computation.7 | async-start | bytes 2097152 | tf_op jit(solution)/shard_map/all_to_all | solution.py:51
  502.1 27.6 %copy-start.16 = (f32[512]{0:T(512)S(1)}, f32[512]{0:T(512)}, u32[]{:S(2)}) copy-start(f32[512]{0:T(512)} %param.26) | copy-start | bytes 6148
  541.6 35.4 %copy-start.18 = (s32[128]{0:T(128)S(1)}, s32[128]{0:T(128)}, u32[]{:S(2)}) copy-start(s32[128]{0:T(128)} %param.17) | copy-start | bytes 1540
  543.2 33.8 %all-to-all-start.8 = ((bf16[16,8,8192]{2,1,0:T(8,128)(2,1)}), bf16[16,8,8192]{2,1,0:T(8,128)(2,1)S(1)}, u32[]{:S(2)}, u32[]{:S(2)}) async-start(bf16[16,8,8192]{2,1,0:T(8,128)(2,1)} %broadcast_in_dim.24), calls=%async_computation.8 | async-start | bytes 4194304 | tf_op jit(solution)/shard_map/all_to_all | solution.py:51
Sparse Core Ops, SparseCore 0:
  10.5 50.6 all-gather.6
  63.7 47.4 all-gather.8
